TPU v7x, 512 devices: a whole 4x4x16 slice. The times are simulated.
512 devices in a mesh: blk: 8 (over y, x_hi), grp: 64 (over z, x_lo, core).
Axes of the slice: x: 4 (x_hi: 2, x_lo: 2; x = x_hi * 2 + x_lo), y: 4, z: 16, core: 2. Of those that a mesh axis runs over, the one named last changes fastest.
Arguments:
- positions: float32 [3, 131072], P(None, ('blk', 'grp')), may hold values from -6 to 6
- velocities: float32 [3, 131072], P(None, ('blk', 'grp')), may hold values from -6 to 6
- accelerations: float32 [3, 131072], P(None, ('blk', 'grp')), may hold values from -4 to 4
- jerks: float32 [3, 131072], P(None, ('blk', 'grp')), may hold values from -4 to 4
- mass_weight: float32 [131072], P(('blk', 'grp')), may hold values from 0.3 to 3
- levels: int32 [131072], P(('blk', 'grp')), may hold values from 0 to 3, as said below
- active: int32 [2, 12288], P(None, ('blk', 'grp')), may hold values from 0 to 255, as said below
- counts: int32 [2, 512], P(None, ('blk', 'grp')), may hold values from 1 to 24
Outputs:
- positions_out: float32 [3, 131072], P(None, ('blk', 'grp'))
- velocities_out: float32 [3, 131072], P(None, ('blk', 'grp'))
- accelerations_out: float32 [3, 131072], P(None, ('blk', 'grp'))
- jerks_out: float32 [3, 131072], P(None, ('blk', 'grp'))
- fresh_forces: float32 [2, 6, 12288], P(None, None, ('blk', 'grp'))
Inputs may be any that keep to these rules, and one draw needn't show every extreme that they name: `active`: entries are local indices of the owner's particles; the live slots of one owner's list are distinct, dead slots hold 0. `levels`: particles not named in any list have level 2 or 3.
All inputs are finite; a program needn't handle non-finite values.
Results may differ from a plain program's by a relative error of at most 0.0003.
Values sent between devices are 32-bit elements; how exact they have to be, the bound alone decides.
No kernel may reach another device: no remote copies, remote signals or barrier semaphores. Data moves between devices by JAX's collectives and lax.ppermute only.
A program may use at most 64 MiB of HBM per device.

v0:
```python
import jax
import jax.numpy as jnp
from jax import lax
from jax.sharding import PartitionSpec as P

STEP_BASE = 0.125
SOFTEN = 0.01


def passed_along(value, axis, steps):
    count = lax.axis_size(axis)
    pairs = [(source, (source + steps) % count) for source in range(count)]
    return lax.ppermute(value, axis, pairs)


def predict(pos, vel, acc, jerk, elapsed):
    pred_pos = pos + elapsed * (vel + elapsed * (acc * 0.5 + elapsed * jerk / 6.0))
    pred_vel = vel + elapsed * (acc + elapsed * jerk * 0.5)
    return (pred_pos, pred_vel)


def correct(pos, vel, acc, jerk, new_acc, new_jerk, stride, hit):
    half = 0.5 * stride
    square = stride * stride / 12.0
    vel_new = vel + half * (acc + new_acc) + square * (jerk - new_jerk)
    pos_new = pos + half * (vel + vel_new) + square * (acc - new_acc)
    return (
        jnp.where(hit, pos_new, pos),
        jnp.where(hit, vel_new, vel),
        jnp.where(hit, new_acc, acc),
        jnp.where(hit, new_jerk, jerk),
    )


def block_terms(iblock, jpart):
    dpos = jpart[0:3, :, None] - iblock[0:3, None, :]
    dvel = jpart[3:6, :, None] - iblock[3:6, None, :]
    dist = dpos[0] * dpos[0] + dpos[1] * dpos[1] + dpos[2] * dpos[2] + SOFTEN
    inverse = lax.rsqrt(dist)
    weight = jpart[6][:, None] * inverse * inverse * inverse
    radial = 3.0 * (dpos[0] * dvel[0] + dpos[1] * dvel[1] + dpos[2] * dvel[2]) * inverse * inverse
    accel = jnp.sum(weight[None] * dpos, axis=1)
    jerk = jnp.sum(weight[None] * (dvel - radial[None] * dpos), axis=1)
    return jnp.concatenate([accel, jerk], axis=0)


def pair_terms(ipart, jpart):
    rows = ipart.shape[1]
    width = 512
    blocks = ipart.reshape(6, rows // width, width).transpose(1, 0, 2)
    result = lax.map(lambda iblock: block_terms(iblock, jpart), blocks)
    return result.transpose(1, 0, 2).reshape(6, rows)


def body(positions, velocities, accelerations, jerks, mass_weight, levels, active, counts):
    count_part = positions.shape[1]
    loop_len = lax.axis_size("blk")
    total_part = count_part * loop_len * lax.axis_size("grp")
    mass = mass_weight / total_part
    clock = jnp.zeros((count_part,), jnp.float32)
    stride = STEP_BASE * jnp.left_shift(jnp.ones_like(levels), levels).astype(jnp.float32)
    particle = jnp.arange(count_part, dtype=jnp.int32)
    slot = jnp.arange(active.shape[1], dtype=jnp.int32)
    pos, vel, acc, jerk = (positions, velocities, accelerations, jerks)
    recorded = []
    for step in range(2):
        now = STEP_BASE * (step + 1)
        elapsed = now - clock
        pred_pos, pred_vel = predict(pos, vel, acc, jerk, elapsed)
        live = slot < counts[step, 0]
        picker = ((active[step][:, None] == particle[None, :]) & live[:, None]).astype(jnp.float32)
        pred_both = jnp.concatenate([pred_pos, pred_vel], axis=0)
        chosen = jnp.dot(pred_both, picker.T, precision=lax.Precision.HIGHEST)
        jdata = jnp.concatenate([pred_pos, pred_vel, mass[None, :]], axis=0)
        row_actives = lax.all_gather(chosen, "grp", axis=1, tiled=True)
        travel = jdata
        partial_value = pair_terms(row_actives, travel)
        for turn in range(loop_len - 1):
            travel = passed_along(travel, "blk", 1)
            partial_value = partial_value + pair_terms(row_actives, travel)
        fresh = lax.psum_scatter(partial_value, "grp", scatter_dimension=1, tiled=True)
        recorded.append(jnp.where(live[None, :], fresh, jnp.zeros_like(fresh)))
        spread = jnp.dot(fresh, picker, precision=lax.Precision.HIGHEST)
        hit = jnp.sum(picker, axis=0) > 0.5
        pos, vel, acc, jerk = correct(pos, vel, acc, jerk, spread[0:3], spread[3:6], stride, hit)
        clock = jnp.where(hit, now, clock)
    return (pos, vel, acc, jerk, jnp.stack(recorded))


def solution(mesh):
    in_specs = (
        P(None, ("blk", "grp")),
        P(None, ("blk", "grp")),
        P(None, ("blk", "grp")),
        P(None, ("blk", "grp")),
        P(("blk", "grp")),
        P(("blk", "grp")),
        P(None, ("blk", "grp")),
        P(None, ("blk", "grp")),
    )
    out_specs = (
        P(None, ("blk", "grp")),
        P(None, ("blk", "grp")),
        P(None, ("blk", "grp")),
        P(None, ("blk", "grp")),
        P(None, None, ("blk", "grp")),
    )
    return jax.shard_map(body, mesh=mesh, in_specs=in_specs, out_specs=out_specs, check_vma=False)
```

profile of v0, /device:TPU:8, one launch (start us, length us, event | category | flops | bytes accessed | tf_op | source)
XLA Modules:
  0.0 726.7 jit_solution(7980893641859117160)
XLA Ops:
  2.1 4.9 collective-permute-start
  10.0 69.5 %all-gather = f32[64,24,6]{1,2,0:T(8,128)S(1)} all-gather(f32[1,24,6]{1,2,0:T(8,128)S(1)} %convolution_bitcast_fusion.1), channel_id=1, replica_groups=mesh['blk'=8,'grp'=64] {'grp'}, dimensions={0}, use_global_device_ids=true | all-gather | bytes 37440 | tf_op jit(solution)/shard_map/all_gather | solution.py:75
  86.8 5.0 collective-permute-start.1
  91.7 8.1 %while.161 = (s32[]{:T(128)}, f32[3,6,512]{2,1,0:T(8,128)S(1)}, f32[7,256]{1,0:T(8,128)}, f32[3,6,512]{2,1,0:T(8,128)S(1)}, s32[]{:T(128)}, /*index=5*/s32[]{:T(128)}, s32[]{}) while((s32[]{:T(128)}, f32[3,6,512]{2,1,0:T(8,128)S(1)}, f32[7,256]{1,0:T(8,128)}, f32[3,6,512]{2,1,0:T(8,128)S(1)}, s32[]{:T(128)}, /*index=5*/s32[]{:T(128)}, ...), condition=%wide.region_9.10_spmd, body=%wide.region_6.9_spmd.sunk | while | flops 6160387 | bytes 8510565 | solution.py:51
  103.2 8.1 %while.162 = (s32[]{:T(128)}, f32[3,6,512]{2,1,0:T(8,128)S(1)}, f32[7,256]{1,0:T(8,128)}, f32[3,6,512]{2,1,0:T(8,128)S(1)}, s32[]{:T(128)}, /*index=5*/s32[]{:T(128)}, s32[]{}) while((s32[]{:T(128)}, f32[3,6,512]{2,1,0:T(8,128)S(1)}, f32[7,256]{1,0:T(8,128)}, f32[3,6,512]{2,1,0:T(8,128)S(1)}, s32[]{:T(128)}, /*index=5*/s32[]{:T(128)}, ...), condition=%wide.region_13.14_spmd, body=%wide.region_10.13_spmd.sunk | while | flops 6160387 | bytes 8510565 | solution.py:51
  111.4 4.7 collective-permute-start.3
  116.1 8.1 %while.163 = (s32[]{:T(128)}, f32[3,6,512]{2,1,0:T(8,128)S(1)}, f32[7,256]{1,0:T(8,128)}, f32[3,6,512]{2,1,0:T(8,128)S(1)}, s32[]{:T(128)}, /*index=5*/s32[]{:T(128)}, s32[]{}) while((s32[]{:T(128)}, f32[3,6,512]{2,1,0:T(8,128)S(1)}, f32[7,256]{1,0:T(8,128)}, f32[3,6,512]{2,1,0:T(8,128)S(1)}, s32[]{:T(128)}, /*index=5*/s32[]{:T(128)}, ...), condition=%wide.region_17.18_spmd, body=%wide.region_14.17_spmd.sunk | while | flops 6160387 | bytes 8510565 | solution.py:51
  127.6 8.1 %while.164 = (s32[]{:T(128)}, f32[3,6,512]{2,1,0:T(8,128)S(1)}, f32[7,256]{1,0:T(8,128)}, f32[3,6,512]{2,1,0:T(8,128)S(1)}, s32[]{:T(128)}, /*index=5*/s32[]{:T(128)}, s32[]{}) while((s32[]{:T(128)}, f32[3,6,512]{2,1,0:T(8,128)S(1)}, f32[7,256]{1,0:T(8,128)}, f32[3,6,512]{2,1,0:T(8,128)S(1)}, s32[]{:T(128)}, /*index=5*/s32[]{:T(128)}, ...), condition=%wide.region_21.22_spmd, body=%wide.region_18.21_spmd.sunk | while | flops 6160387 | bytes 8510565 | solution.py:51
  139.4 8.1 %while.165 = (s32[]{:T(128)}, f32[3,6,512]{2,1,0:T(8,128)S(1)}, f32[7,256]{1,0:T(8,128)}, f32[3,6,512]{2,1,0:T(8,128)S(1)}, s32[]{:T(128)}, /*index=5*/s32[]{:T(128)}, s32[]{}) while((s32[]{:T(128)}, f32[3,6,512]{2,1,0:T(8,128)S(1)}, f32[7,256]{1,0:T(8,128)}, f32[3,6,512]{2,1,0:T(8,128)S(1)}, s32[]{:T(128)}, /*index=5*/s32[]{:T(128)}, ...), condition=%wide.region_25.26_spmd, body=%wide.region_22.25_spmd.sunk | while | flops 6160387 | bytes 8510565 | solution.py:51
  150.9 8.1 %while.166 = (s32[]{:T(128)}, f32[3,6,512]{2,1,0:T(8,128)S(1)}, f32[7,256]{1,0:T(8,128)}, f32[3,6,512]{2,1,0:T(8,128)S(1)}, s32[]{:T(128)}, /*index=5*/s32[]{:T(128)}, s32[]{}) while((s32[]{:T(128)}, f32[3,6,512]{2,1,0:T(8,128)S(1)}, f32[7,256]{1,0:T(8,128)}, f32[3,6,512]{2,1,0:T(8,128)S(1)}, s32[]{:T(128)}, /*index=5*/s32[]{:T(128)}, ...), condition=%wide.region_29.30_spmd, body=%wide.region_26.29_spmd.sunk | while | flops 6160387 | bytes 8510565 | solution.py:51
  159.0 3.7 while.167
  162.8 207.4 %all-reduce = f32[6,1536]{1,0:T(8,128)S(1)} all-reduce(f32[6,1536]{1,0:T(8,128)S(1)} %bitcast.364), channel_id=2, replica_groups=mesh['blk'=8,'grp'=64] {'grp'}, use_global_device_ids=true, to_apply=%region_34.35.clone | all-reduce | flops 9216 | bytes 73728
  370.7 60.2 %all-gather.1 = f32[64,24,6]{1,2,0:T(8,128)S(1)} all-gather(f32[1,24,6]{1,2,0:T(8,128)S(1)} %convolution_bitcast_fusion), channel_id=1, replica_groups=mesh['blk'=8,'grp'=64] {'grp'}, dimensions={0}, use_global_device_ids=true | all-gather | bytes 37440 | tf_op jit(solution)/shard_map/all_gather | solution.py:75
  431.1 5.0 collective-permute-start.7
  443.3 8.1 %while.169 = (s32[]{:T(128)}, f32[3,6,512]{2,1,0:T(8,128)S(1)}, f32[7,256]{1,0:T(8,128)}, f32[3,6,512]{2,1,0:T(8,128)S(1)}, s32[]{:T(128)}, /*index=5*/s32[]{:T(128)}, s32[]{}) while((s32[]{:T(128)}, f32[3,6,512]{2,1,0:T(8,128)S(1)}, f32[7,256]{1,0:T(8,128)}, f32[3,6,512]{2,1,0:T(8,128)S(1)}, s32[]{:T(128)}, /*index=5*/s32[]{:T(128)}, ...), condition=%wide.region_42.43_spmd, body=%wide.region_39.42_spmd.sunk | while | flops 6160387 | bytes 8510565 | solution.py:51
  451.4 5.0 collective-permute-start.9
  456.4 8.1 %while.170 = (s32[]{:T(128)}, f32[3,6,512]{2,1,0:T(8,128)S(1)}, f32[7,256]{1,0:T(8,128)}, f32[3,6,512]{2,1,0:T(8,128)S(1)}, s32[]{:T(128)}, /*index=5*/s32[]{:T(128)}, s32[]{}) while((s32[]{:T(128)}, f32[3,6,512]{2,1,0:T(8,128)S(1)}, f32[7,256]{1,0:T(8,128)}, f32[3,6,512]{2,1,0:T(8,128)S(1)}, s32[]{:T(128)}, /*index=5*/s32[]{:T(128)}, ...), condition=%wide.region_46.47_spmd, body=%wide.region_43.46_spmd.sunk | while | flops 6160387 | bytes 8510565 | solution.py:51
  467.9 8.1 %while.171 = (s32[]{:T(128)}, f32[3,6,512]{2,1,0:T(8,128)S(1)}, f32[7,256]{1,0:T(8,128)}, f32[3,6,512]{2,1,0:T(8,128)S(1)}, s32[]{:T(128)}, /*index=5*/s32[]{:T(128)}, s32[]{}) while((s32[]{:T(128)}, f32[3,6,512]{2,1,0:T(8,128)S(1)}, f32[7,256]{1,0:T(8,128)}, f32[3,6,512]{2,1,0:T(8,128)S(1)}, s32[]{:T(128)}, /*index=5*/s32[]{:T(128)}, ...), condition=%wide.region_50.51_spmd, body=%wide.region_47.50_spmd.sunk | while | flops 6160387 | bytes 8510565 | solution.py:51
  476.1 4.7 collective-permute-start.11
  480.8 8.1 %while.172 = (s32[]{:T(128)}, f32[3,6,512]{2,1,0:T(8,128)S(1)}, f32[7,256]{1,0:T(8,128)}, f32[3,6,512]{2,1,0:T(8,128)S(1)}, s32[]{:T(128)}, /*index=5*/s32[]{:T(128)}, s32[]{}) while((s32[]{:T(128)}, f32[3,6,512]{2,1,0:T(8,128)S(1)}, f32[7,256]{1,0:T(8,128)}, f32[3,6,512]{2,1,0:T(8,128)S(1)}, s32[]{:T(128)}, /*index=5*/s32[]{:T(128)}, ...), condition=%wide.region_54.55_spmd, body=%wide.region_51.54_spmd.sunk | while | flops 6160387 | bytes 8510565 | solution.py:51
  492.3 8.1 %while.173 = (s32[]{:T(128)}, f32[3,6,512]{2,1,0:T(8,128)S(1)}, f32[7,256]{1,0:T(8,128)}, f32[3,6,512]{2,1,0:T(8,128)S(1)}, s32[]{:T(128)}, /*index=5*/s32[]{:T(128)}, s32[]{}) while((s32[]{:T(128)}, f32[3,6,512]{2,1,0:T(8,128)S(1)}, f32[7,256]{1,0:T(8,128)}, f32[3,6,512]{2,1,0:T(8,128)S(1)}, s32[]{:T(128)}, /*index=5*/s32[]{:T(128)}, ...), condition=%wide.region_58.59_spmd, body=%wide.region_55.58_spmd.sunk | while | flops 6160387 | bytes 8510565 | solution.py:51
  500.4 5.5 collective-permute-start.13
  505.9 8.1 %while.174 = (s32[]{:T(128)}, f32[3,6,512]{2,1,0:T(8,128)S(1)}, f32[7,256]{1,0:T(8,128)}, f32[3,6,512]{2,1,0:T(8,128)S(1)}, s32[]{:T(128)}, /*index=5*/s32[]{:T(128)}, s32[]{}) while((s32[]{:T(128)}, f32[3,6,512]{2,1,0:T(8,128)S(1)}, f32[7,256]{1,0:T(8,128)}, f32[3,6,512]{2,1,0:T(8,128)S(1)}, s32[]{:T(128)}, /*index=5*/s32[]{:T(128)}, ...), condition=%wide.region_62.63_spmd, body=%wide.region_59.62_spmd.sunk | while | flops 6160387 | bytes 8510565 | solution.py:51
  517.8 207.4 %all-reduce.1 = f32[6,1536]{1,0:T(8,128)S(1)} all-reduce(f32[6,1536]{1,0:T(8,128)S(1)} %bitcast.365), channel_id=3, replica_groups=mesh['blk'=8,'grp'=64] {'grp'}, use_global_device_ids=true, to_apply=%region_67.68.clone | all-reduce | flops 9216 | bytes 73728
  (411 shorter events, 154.7 us)
Async XLA Ops:
  2.1 84.7 %collective-permute-start = (f32[7,256]{1,0:T(8,128)S(1)}, f32[7,256]{1,0:T(8,128)}, u32[]{:S(2)}, u32[]{:S(2)}) collective-permute-start(f32[7,256]{1,0:T(8,128)S(1)} %pad_maximum_fusion.1), channel_id=1, source_target_pairs={{0,64},{64,128},{128,192},{192,256},{256,320},{320,384},{384,448},... | collective-permute-start | bytes 21512 | tf_op jit(solution)/shard_map/ppermute | solution.py:13
  79.8 3.7 copy-start.4
  86.8 13.1 %collective-permute-start.1 = (f32[7,256]{1,0:T(8,128)}, f32[7,256]{1,0:T(8,128)}, u32[]{:S(2)}, u32[]{:S(2)}) collective-permute-start(f32[7,256]{1,0:T(8,128)} %collective-permute-done), channel_id=1, source_target_pairs={{0,64},{64,128},{128,192},{192,256},{256,320},{320,384},{384,448},... | collective-permute-start | bytes 21512 | tf_op jit(solution)/shard_map/ppermute | solution.py:13
  99.8 11.5 %collective-permute-start.2 = (f32[7,256]{1,0:T(8,128)}, f32[7,256]{1,0:T(8,128)}, u32[]{:S(2)}, u32[]{:S(2)}) collective-permute-start(f32[7,256]{1,0:T(8,128)} %collective-permute-done.1), channel_id=1, source_target_pairs={{0,64},{64,128},{128,192},{192,256},{256,320},{320,384},{384,448},... | collective-permute-start | bytes 21512 | tf_op jit(solution)/shard_map/ppermute | solution.py:13
  111.4 12.8 %collective-permute-start.3 = (f32[7,256]{1,0:T(8,128)}, f32[7,256]{1,0:T(8,128)}, u32[]{:S(2)}, u32[]{:S(2)}) collective-permute-start(f32[7,256]{1,0:T(8,128)} %collective-permute-done.2), channel_id=1, source_target_pairs={{0,64},{64,128},{128,192},{192,256},{256,320},{320,384},{384,448},... | collective-permute-start | bytes 21512 | tf_op jit(solution)/shard_map/ppermute | solution.py:13
  124.2 11.5 %collective-permute-start.4 = (f32[7,256]{1,0:T(8,128)}, f32[7,256]{1,0:T(8,128)}, u32[]{:S(2)}, u32[]{:S(2)}) collective-permute-start(f32[7,256]{1,0:T(8,128)} %collective-permute-done.3), channel_id=1, source_target_pairs={{0,64},{64,128},{128,192},{192,256},{256,320},{320,384},{384,448},... | collective-permute-start | bytes 21512 | tf_op jit(solution)/shard_map/ppermute | solution.py:13
  135.7 11.8 %collective-permute-start.5 = (f32[7,256]{1,0:T(8,128)}, f32[7,256]{1,0:T(8,128)}, u32[]{:S(2)}, u32[]{:S(2)}) collective-permute-start(f32[7,256]{1,0:T(8,128)} %collective-permute-done.4), channel_id=1, source_target_pairs={{0,64},{64,128},{128,192},{192,256},{256,320},{320,384},{384,448},... | collective-permute-start | bytes 21512 | tf_op jit(solution)/shard_map/ppermute | solution.py:13
  147.5 11.5 %collective-permute-start.6 = (f32[7,256]{1,0:T(8,128)}, f32[7,256]{1,0:T(8,128)S(1)}, u32[]{:S(2)}, u32[]{:S(2)}) collective-permute-start(f32[7,256]{1,0:T(8,128)} %collective-permute-done.5), channel_id=1, source_target_pairs={{0,64},{64,128},{128,192},{192,256},{256,320},{320,384},{384,448},... | collective-permute-start | bytes 21512 | tf_op jit(solution)/shard_map/ppermute | solution.py:13
  159.0 211.4 %copy-start = (f32[3,256]{1,0:T(4,128)S(1)}, f32[3,256]{1,0:T(4,128)}, u32[]{:S(2)}) copy-start(f32[3,256]{1,0:T(4,128)} %param.43) | copy-start | bytes 9220
  159.0 211.4 %copy-start.1 = (f32[3,256]{1,0:T(4,128)S(1)}, f32[3,256]{1,0:T(4,128)}, u32[]{:S(2)}) copy-start(f32[3,256]{1,0:T(4,128)} %param.40) | copy-start | bytes 9220
  159.0 211.4 %copy-start.2 = (f32[3,256]{1,0:T(4,128)S(1)}, f32[3,256]{1,0:T(4,128)}, u32[]{:S(2)}) copy-start(f32[3,256]{1,0:T(4,128)} %param.41) | copy-start | bytes 9220
  159.0 211.4 %copy-start.3 = (f32[3,256]{1,0:T(4,128)S(1)}, f32[3,256]{1,0:T(4,128)}, u32[]{:S(2)}) copy-start(f32[3,256]{1,0:T(4,128)} %param.42) | copy-start | bytes 9220
  431.1 8.8 %collective-permute-start.7 = (f32[7,256]{1,0:T(8,128)S(1)}, f32[7,256]{1,0:T(8,128)}, u32[]{:S(2)}, u32[]{:S(2)}) collective-permute-start(f32[7,256]{1,0:T(8,128)S(1)} %pad_maximum_fusion), channel_id=1, source_target_pairs={{0,64},{64,128},{128,192},{192,256},{256,320},{320,384},{384,448},... | collective-permute-start | bytes 21512 | tf_op jit(solution)/shard_map/ppermute | solution.py:13
  439.9 11.5 %collective-permute-start.8 = (f32[7,256]{1,0:T(8,128)}, f32[7,256]{1,0:T(8,128)}, u32[]{:S(2)}, u32[]{:S(2)}) collective-permute-start(f32[7,256]{1,0:T(8,128)} %collective-permute-done.7), channel_id=1, source_target_pairs={{0,64},{64,128},{128,192},{192,256},{256,320},{320,384},{384,448},... | collective-permute-start | bytes 21512 | tf_op jit(solution)/shard_map/ppermute | solution.py:13
  451.4 13.1 %collective-permute-start.9 = (f32[7,256]{1,0:T(8,128)}, f32[7,256]{1,0:T(8,128)}, u32[]{:S(2)}, u32[]{:S(2)}) collective-permute-start(f32[7,256]{1,0:T(8,128)} %collective-permute-done.8), channel_id=1, source_target_pairs={{0,64},{64,128},{128,192},{192,256},{256,320},{320,384},{384,448},... | collective-permute-start | bytes 21512 | tf_op jit(solution)/shard_map/ppermute | solution.py:13
  464.5 11.5 %collective-permute-start.10 = (f32[7,256]{1,0:T(8,128)}, f32[7,256]{1,0:T(8,128)}, u32[]{:S(2)}, u32[]{:S(2)}) collective-permute-start(f32[7,256]{1,0:T(8,128)} %collective-permute-done.9), channel_id=1, source_target_pairs={{0,64},{64,128},{128,192},{192,256},{256,320},{320,384},{384,448},... | collective-permute-start | bytes 21512 | tf_op jit(solution)/shard_map/ppermute | solution.py:13
  476.1 12.8 %collective-permute-start.11 = (f32[7,256]{1,0:T(8,128)}, f32[7,256]{1,0:T(8,128)}, u32[]{:S(2)}, u32[]{:S(2)}) collective-permute-start(f32[7,256]{1,0:T(8,128)} %collective-permute-done.10), channel_id=1, source_target_pairs={{0,64},{64,128},{128,192},{192,256},{256,320},{320,384},{384,448},... | collective-permute-start | bytes 21512 | tf_op jit(solution)/shard_map/ppermute | solution.py:13
  488.9 11.5 %collective-permute-start.12 = (f32[7,256]{1,0:T(8,128)}, f32[7,256]{1,0:T(8,128)}, u32[]{:S(2)}, u32[]{:S(2)}) collective-permute-start(f32[7,256]{1,0:T(8,128)} %collective-permute-done.11), channel_id=1, source_target_pairs={{0,64},{64,128},{128,192},{192,256},{256,320},{320,384},{384,448},... | collective-permute-start | bytes 21512 | tf_op jit(solution)/shard_map/ppermute | solution.py:13
  500.4 13.6 %collective-permute-start.13 = (f32[7,256]{1,0:T(8,128)}, f32[7,256]{1,0:T(8,128)S(1)}, u32[]{:S(2)}, u32[]{:S(2)}) collective-permute-start(f32[7,256]{1,0:T(8,128)} %collective-permute-done.12), channel_id=1, source_target_pairs={{0,64},{64,128},{128,192},{192,256},{256,320},{320,384},{384,448},... | collective-permute-start | bytes 21512 | tf_op jit(solution)/shard_map/ppermute | solution.py:13
  514.0 212.1 %copy-start.5 = (pred[256]{0:T(512)(128)(4,1)S(1)}, pred[256]{0:T(512)(128)(4,1)}, u32[]{:S(2)}) copy-start(pred[256]{0:T(512)(128)(4,1)} %broadcast_compare_fusion.1) | copy-start | bytes 772
where the time goes:
time: 733 us; the launch traced here: 727 us
  blocking collectives  544 us (74%)
  other arithmetic  60.6 us (8%)
  starting transfers between devices  58.6 us (8%)
  local copies, waits for them, and re-layouts  58.3 us (8%)
    unnamed x2, blocking collectives  415 us
    all_gather x2, blocking collectives, body(): row_actives = lax.all_gather(chosen, 'grp', axis=1, tiled=True)  130 us
    ppermute x14, starting transfers between devices, passed_along(): return lax.ppermute(value, axis, pairs)  58.6 us
    slice x42, local copies, waits for them, and re-layouts, block_terms(): dvel = jpart[3:6, :, None] - iblock[3:6, None, :]  27.9 us
    reduce_sum x48, other arithmetic, block_terms(): accel = jnp.sum(weight[None] * dpos, axis=1)  27.4 us
    slice x42, local copies, waits for them, and re-layouts, block_terms(): weight = jpart[6][:, None] * inverse * inverse * inverse  25.3 us
    mul x48, other arithmetic, block_terms(): jerk = jnp.sum(weight[None] * (dvel - radial[None] * dpos), axis=1)  15.3 us
  transfers between devices with their start and end apart: 14, of which 0 were waited for; matrix products, arithmetic and copies ran while one was open for 15% of the time, Pallas kernels for 0%

commit v1 on v0

--- a/solution.py
+++ b/solution.py
@@ -72,7 +72,9 @@
         pred_both = jnp.concatenate([pred_pos, pred_vel], axis=0)
         chosen = jnp.dot(pred_both, picker.T, precision=lax.Precision.HIGHEST)
         jdata = jnp.concatenate([pred_pos, pred_vel, mass[None, :]], axis=0)
-        row_actives = lax.all_gather(chosen, "grp", axis=1, tiled=True)
+        row_actives = jnp.concatenate(
+            lax.all_to_all(jnp.stack([chosen] * lax.axis_size("grp")), "grp", 0, 0), axis=1
+        )
         travel = jdata
         partial_value = pair_terms(row_actives, travel)
         for turn in range(loop_len - 1):

time: 733 us -> 628 us (0.86)
  the two profiles are of different devices: /device:TPU:8 before, /device:TPU:28 now
where the time goes in v1:
time: 628 us; the launch traced here: 626 us
  blocking collectives  416 us (66%)
  starting transfers between devices  99.7 us (16%)
  other arithmetic  62.3 us (10%)
  waiting for transfers between devices  26.4 us (4%)
  local copies, waits for them, and re-layouts  16.7 us (3%)
    unnamed x2, blocking collectives  416 us
    ppermute x14, starting transfers between devices, passed_along(): return lax.ppermute(value, axis, pairs)  75.3 us
    reduce_sum x48, other arithmetic, block_terms(): accel = jnp.sum(weight[None] * dpos, axis=1)  27.4 us
    all_to_all x2, starting transfers between devices, body(): lax.all_to_all(jnp.stack([chosen] * lax.axis_size('grp')), 'grp', 0, 0)  24.4 us
    ppermute x14, waiting for transfers between devices, passed_along(): return lax.ppermute(value, axis, pairs)  23.3 us
    mul x48, other arithmetic, block_terms(): jerk = jnp.sum(weight[None] * (dvel - radial[None] * dpos), axis=1)  15.2 us
    sub x48, other arithmetic, block_terms(): dvel = jpart[3:6, :, None] - iblock[3:6, None, :]  12.9 us
  transfers between devices with their start and end apart: 16, of which 9 were waited for; matrix products, arithmetic and copies ran while one was open for 8% of the time, Pallas kernels for 0%

profile of v1, /device:TPU:28, one launch (start us, length us, event | category | flops | bytes accessed | tf_op | source)
XLA Modules:
  0.0 626.3 jit_solution(12382770390779178479)
XLA Ops:
  2.1 7.4 %collective-permute-start = (f32[7,256]{1,0:T(8,128)S(1)}, f32[7,256]{1,0:T(8,128)S(1)}, u32[]{:S(2)}, u32[]{:S(2)}) collective-permute-start(f32[7,256]{1,0:T(8,128)S(1)} %pad_maximum_fusion.1), channel_id=1, source_target_pairs={{0,64},{64,128},{128,192},{192,256},{256,320},{320,384},{384,448},... | collective-permute-start | bytes 21512 | tf_op jit(solution)/shard_map/ppermute | solution.py:13
  11.6 7.1 %collective-permute-start.1 = (f32[7,256]{1,0:T(8,128)S(1)}, f32[7,256]{1,0:T(8,128)S(1)}, u32[]{:S(2)}, u32[]{:S(2)}) collective-permute-start(f32[7,256]{1,0:T(8,128)S(1)} %collective-permute-done), channel_id=1, source_target_pairs={{0,64},{64,128},{128,192},{192,256},{256,320},{320,384},{384,448},... | collective-permute-start | bytes 21512 | tf_op jit(solution)/shard_map/ppermute | solution.py:13
  20.0 7.8 %collective-permute-start.2 = (f32[7,256]{1,0:T(8,128)S(1)}, f32[7,256]{1,0:T(8,128)S(1)}, u32[]{:S(2)}, u32[]{:S(2)}) collective-permute-start(f32[7,256]{1,0:T(8,128)S(1)} %collective-permute-done.1), channel_id=1, source_target_pairs={{0,64},{64,128},{128,192},{192,256},{256,320},{320,384},{384,448},... | collective-permute-start | bytes 21512 | tf_op jit(solution)/shard_map/ppermute | solution.py:13
  28.9 12.3 %all-to-all-start = ((f32[64,1,144]{2,1,0:T(1,128)}), f32[64,1,144]{2,1,0:T(1,128)S(1)}, u32[]{:S(2)}, u32[]{:S(2)}) async-start(f32[64,1,144]{2,1,0:T(1,128)} %reshape.339), calls=%async_computation | async-start | bytes 131072 | tf_op jit(solution)/shard_map/all_to_all | solution.py:76
  43.8 4.4 collective-permute-done.3
  48.2 4.0 collective-permute-start.4
  55.2 6.1 collective-permute-start.5
  63.3 7.3 %collective-permute-start.6 = (f32[7,256]{1,0:T(8,128)}, f32[7,256]{1,0:T(8,128)S(1)}, u32[]{:S(2)}, u32[]{:S(2)}) collective-permute-start(f32[7,256]{1,0:T(8,128)} %collective-permute-done.5), channel_id=1, source_target_pairs={{0,64},{64,128},{128,192},{192,256},{256,320},{320,384},{384,448},... | collective-permute-start | bytes 21512 | tf_op jit(solution)/shard_map/ppermute | solution.py:13
  72.3 8.1 %while.166 = (s32[]{:T(128)}, f32[3,6,512]{2,1,0:T(8,128)S(1)}, f32[7,256]{1,0:T(8,128)}, f32[3,6,512]{2,1,0:T(8,128)S(1)}, s32[]{:T(128)}, /*index=5*/s32[]{:T(128)}, s32[]{}) while((s32[]{:T(128)}, f32[3,6,512]{2,1,0:T(8,128)S(1)}, f32[7,256]{1,0:T(8,128)}, f32[3,6,512]{2,1,0:T(8,128)S(1)}, s32[]{:T(128)}, /*index=5*/s32[]{:T(128)}, ...), condition=%wide.region_29.30_spmd, body=%wide.region_26.29_spmd.sunk | while | flops 6160387 | bytes 8510565 | solution.py:51
  91.8 3.8 while.163
  95.5 3.8 while.162
  99.3 3.8 while.161
  106.8 208.1 %all-reduce = f32[6,1536]{1,0:T(8,128)S(1)} all-reduce(f32[6,1536]{1,0:T(8,128)S(1)} %bitcast.358), channel_id=2, replica_groups=mesh['blk'=8,'grp'=64] {'grp'}, use_global_device_ids=true, to_apply=%region_34.35.clone | all-reduce | flops 9216 | bytes 73728
  317.2 5.1 collective-permute-done.7
  322.3 4.0 collective-permute-start.8
  329.4 6.1 collective-permute-start.9
  336.8 7.8 %collective-permute-start.10 = (f32[7,256]{1,0:T(8,128)S(1)}, f32[7,256]{1,0:T(8,128)S(1)}, u32[]{:S(2)}, u32[]{:S(2)}) collective-permute-start(f32[7,256]{1,0:T(8,128)S(1)} %collective-permute-done.9), channel_id=1, source_target_pairs={{0,64},{64,128},{128,192},{192,256},{256,320},{320,384},{384,448},... | collective-permute-start | bytes 21512 | tf_op jit(solution)/shard_map/ppermute | solution.py:13
  346.0 7.8 %collective-permute-start.11 = (f32[7,256]{1,0:T(8,128)S(1)}, f32[7,256]{1,0:T(8,128)S(1)}, u32[]{:S(2)}, u32[]{:S(2)}) collective-permute-start(f32[7,256]{1,0:T(8,128)S(1)} %collective-permute-done.10), channel_id=1, source_target_pairs={{0,64},{64,128},{128,192},{192,256},{256,320},{320,384},{384,448},... | collective-permute-start | bytes 21512 | tf_op jit(solution)/shard_map/ppermute | solution.py:13
  354.8 12.2 %all-to-all-start.1 = ((f32[64,1,144]{2,1,0:T(1,128)}), f32[64,1,144]{2,1,0:T(1,128)S(1)}, u32[]{:S(2)}, u32[]{:S(2)}) async-start(f32[64,1,144]{2,1,0:T(1,128)} %reshape.341), calls=%async_computation.1 | async-start | bytes 131072 | tf_op jit(solution)/shard_map/all_to_all | solution.py:76
  369.0 5.1 collective-permute-done.12
  374.2 4.0 collective-permute-start.13
  390.1 3.8 while.171
  401.4 8.1 %while.174 = (s32[]{:T(128)}, f32[3,6,512]{2,1,0:T(8,128)S(1)}, f32[7,256]{1,0:T(8,128)}, f32[3,6,512]{2,1,0:T(8,128)S(1)}, s32[]{:T(128)}, /*index=5*/s32[]{:T(128)}, s32[]{}) while((s32[]{:T(128)}, f32[3,6,512]{2,1,0:T(8,128)S(1)}, f32[7,256]{1,0:T(8,128)}, f32[3,6,512]{2,1,0:T(8,128)S(1)}, s32[]{:T(128)}, /*index=5*/s32[]{:T(128)}, ...), condition=%wide.region_62.63_spmd, body=%wide.region_59.62_spmd.sunk | while | flops 6160387 | bytes 8510565 | solution.py:51
  417.1 207.8 %all-reduce.1 = f32[6,1536]{1,0:T(8,128)S(1)} all-reduce(f32[6,1536]{1,0:T(8,128)S(1)} %bitcast.359), channel_id=3, replica_groups=mesh['blk'=8,'grp'=64] {'grp'}, use_global_device_ids=true, to_apply=%region_67.68.clone | all-reduce | flops 9216 | bytes 73728
  (416 shorter events, 134.6 us)
Async XLA Ops:
  2.1 9.5 %collective-permute-start = (f32[7,256]{1,0:T(8,128)S(1)}, f32[7,256]{1,0:T(8,128)S(1)}, u32[]{:S(2)}, u32[]{:S(2)}) collective-permute-start(f32[7,256]{1,0:T(8,128)S(1)} %pad_maximum_fusion.1), channel_id=1, source_target_pairs={{0,64},{64,128},{128,192},{192,256},{256,320},{320,384},{384,448},... | collective-permute-start | bytes 21512 | tf_op jit(solution)/shard_map/ppermute | solution.py:13
  11.6 8.4 %collective-permute-start.1 = (f32[7,256]{1,0:T(8,128)S(1)}, f32[7,256]{1,0:T(8,128)S(1)}, u32[]{:S(2)}, u32[]{:S(2)}) collective-permute-start(f32[7,256]{1,0:T(8,128)S(1)} %collective-permute-done), channel_id=1, source_target_pairs={{0,64},{64,128},{128,192},{192,256},{256,320},{320,384},{384,448},... | collective-permute-start | bytes 21512 | tf_op jit(solution)/shard_map/ppermute | solution.py:13
  20.0 21.1 %collective-permute-start.2 = (f32[7,256]{1,0:T(8,128)S(1)}, f32[7,256]{1,0:T(8,128)S(1)}, u32[]{:S(2)}, u32[]{:S(2)}) collective-permute-start(f32[7,256]{1,0:T(8,128)S(1)} %collective-permute-done.1), channel_id=1, source_target_pairs={{0,64},{64,128},{128,192},{192,256},{256,320},{320,384},{384,448},... | collective-permute-start | bytes 21512 | tf_op jit(solution)/shard_map/ppermute | solution.py:13
  28.9 41.8 %all-to-all-start = ((f32[64,1,144]{2,1,0:T(1,128)}), f32[64,1,144]{2,1,0:T(1,128)S(1)}, u32[]{:S(2)}, u32[]{:S(2)}) async-start(f32[64,1,144]{2,1,0:T(1,128)} %reshape.339), calls=%async_computation | async-start | bytes 131072 | tf_op jit(solution)/shard_map/all_to_all | solution.py:76
  41.1 7.0 %collective-permute-start.3 = (f32[7,256]{1,0:T(8,128)S(1)}, f32[7,256]{1,0:T(8,128)S(1)}, u32[]{:S(2)}, u32[]{:S(2)}) collective-permute-start(f32[7,256]{1,0:T(8,128)S(1)} %collective-permute-done.2), channel_id=1, source_target_pairs={{0,64},{64,128},{128,192},{192,256},{256,320},{320,384},{384,448},... | collective-permute-start | bytes 21512 | tf_op jit(solution)/shard_map/ppermute | solution.py:13
  48.2 7.0 %collective-permute-start.4 = (f32[7,256]{1,0:T(8,128)S(1)}, f32[7,256]{1,0:T(8,128)S(1)}, u32[]{:S(2)}, u32[]{:S(2)}) collective-permute-start(f32[7,256]{1,0:T(8,128)S(1)} %collective-permute-done.3), channel_id=1, source_target_pairs={{0,64},{64,128},{128,192},{192,256},{256,320},{320,384},{384,448},... | collective-permute-start | bytes 21512 | tf_op jit(solution)/shard_map/ppermute | solution.py:13
  55.2 8.1 %collective-permute-start.5 = (f32[7,256]{1,0:T(8,128)S(1)}, f32[7,256]{1,0:T(8,128)}, u32[]{:S(2)}, u32[]{:S(2)}) collective-permute-start(f32[7,256]{1,0:T(8,128)S(1)} %collective-permute-done.4), channel_id=1, source_target_pairs={{0,64},{64,128},{128,192},{192,256},{256,320},{320,384},{384,448},... | collective-permute-start | bytes 21512 | tf_op jit(solution)/shard_map/ppermute | solution.py:13
  63.3 17.1 %collective-permute-start.6 = (f32[7,256]{1,0:T(8,128)}, f32[7,256]{1,0:T(8,128)S(1)}, u32[]{:S(2)}, u32[]{:S(2)}) collective-permute-start(f32[7,256]{1,0:T(8,128)} %collective-permute-done.5), channel_id=1, source_target_pairs={{0,64},{64,128},{128,192},{192,256},{256,320},{320,384},{384,448},... | collective-permute-start | bytes 21512 | tf_op jit(solution)/shard_map/ppermute | solution.py:13
  103.1 212.1 %copy-start = (f32[3,256]{1,0:T(4,128)S(1)}, f32[3,256]{1,0:T(4,128)}, u32[]{:S(2)}) copy-start(f32[3,256]{1,0:T(4,128)} %param.43) | copy-start | bytes 9220
  103.1 212.1 %copy-start.1 = (f32[3,256]{1,0:T(4,128)S(1)}, f32[3,256]{1,0:T(4,128)}, u32[]{:S(2)}) copy-start(f32[3,256]{1,0:T(4,128)} %param.40) | copy-start | bytes 9220
  103.1 212.1 %copy-start.2 = (f32[3,256]{1,0:T(4,128)S(1)}, f32[3,256]{1,0:T(4,128)}, u32[]{:S(2)}) copy-start(f32[3,256]{1,0:T(4,128)} %param.41) | copy-start | bytes 9220
  103.1 212.1 %copy-start.3 = (f32[3,256]{1,0:T(4,128)S(1)}, f32[3,256]{1,0:T(4,128)}, u32[]{:S(2)}) copy-start(f32[3,256]{1,0:T(4,128)} %param.42) | copy-start | bytes 9220
  315.3 7.0 %collective-permute-start.7 = (f32[7,256]{1,0:T(8,128)S(1)}, f32[7,256]{1,0:T(8,128)S(1)}, u32[]{:S(2)}, u32[]{:S(2)}) collective-permute-start(f32[7,256]{1,0:T(8,128)S(1)} %pad_maximum_fusion), channel_id=1, source_target_pairs={{0,64},{64,128},{128,192},{192,256},{256,320},{320,384},{384,448},... | collective-permute-start | bytes 21512 | tf_op jit(solution)/shard_map/ppermute | solution.py:13
  322.3 7.0 %collective-permute-start.8 = (f32[7,256]{1,0:T(8,128)S(1)}, f32[7,256]{1,0:T(8,128)S(1)}, u32[]{:S(2)}, u32[]{:S(2)}) collective-permute-start(f32[7,256]{1,0:T(8,128)S(1)} %collective-permute-done.7), channel_id=1, source_target_pairs={{0,64},{64,128},{128,192},{192,256},{256,320},{320,384},{384,448},... | collective-permute-start | bytes 21512 | tf_op jit(solution)/shard_map/ppermute | solution.py:13
  329.4 7.5 %collective-permute-start.9 = (f32[7,256]{1,0:T(8,128)S(1)}, f32[7,256]{1,0:T(8,128)S(1)}, u32[]{:S(2)}, u32[]{:S(2)}) collective-permute-start(f32[7,256]{1,0:T(8,128)S(1)} %collective-permute-done.8), channel_id=1, source_target_pairs={{0,64},{64,128},{128,192},{192,256},{256,320},{320,384},{384,448},... | collective-permute-start | bytes 21512 | tf_op jit(solution)/shard_map/ppermute | solution.py:13
  336.8 9.1 %collective-permute-start.10 = (f32[7,256]{1,0:T(8,128)S(1)}, f32[7,256]{1,0:T(8,128)S(1)}, u32[]{:S(2)}, u32[]{:S(2)}) collective-permute-start(f32[7,256]{1,0:T(8,128)S(1)} %collective-permute-done.9), channel_id=1, source_target_pairs={{0,64},{64,128},{128,192},{192,256},{256,320},{320,384},{384,448},... | collective-permute-start | bytes 21512 | tf_op jit(solution)/shard_map/ppermute | solution.py:13
  346.0 21.0 %collective-permute-start.11 = (f32[7,256]{1,0:T(8,128)S(1)}, f32[7,256]{1,0:T(8,128)S(1)}, u32[]{:S(2)}, u32[]{:S(2)}) collective-permute-start(f32[7,256]{1,0:T(8,128)S(1)} %collective-permute-done.10), channel_id=1, source_target_pairs={{0,64},{64,128},{128,192},{192,256},{256,320},{320,384},{384,448},... | collective-permute-start | bytes 21512 | tf_op jit(solution)/shard_map/ppermute | solution.py:13
  354.8 26.5 %all-to-all-start.1 = ((f32[64,1,144]{2,1,0:T(1,128)}), f32[64,1,144]{2,1,0:T(1,128)S(1)}, u32[]{:S(2)}, u32[]{:S(2)}) async-start(f32[64,1,144]{2,1,0:T(1,128)} %reshape.341), calls=%async_computation.1 | async-start | bytes 131072 | tf_op jit(solution)/shard_map/all_to_all | solution.py:76
  367.0 7.2 %collective-permute-start.12 = (f32[7,256]{1,0:T(8,128)S(1)}, f32[7,256]{1,0:T(8,128)}, u32[]{:S(2)}, u32[]{:S(2)}) collective-permute-start(f32[7,256]{1,0:T(8,128)S(1)} %collective-permute-done.11), channel_id=1, source_target_pairs={{0,64},{64,128},{128,192},{192,256},{256,320},{320,384},{384,448},... | collective-permute-start | bytes 21512 | tf_op jit(solution)/shard_map/ppermute | solution.py:13
  374.2 39.1 %collective-permute-start.13 = (f32[7,256]{1,0:T(8,128)}, f32[7,256]{1,0:T(8,128)S(1)}, u32[]{:S(2)}, u32[]{:S(2)}) collective-permute-start(f32[7,256]{1,0:T(8,128)} %collective-permute-done.12), channel_id=1, source_target_pairs={{0,64},{64,128},{128,192},{192,256},{256,320},{320,384},{384,448},... | collective-permute-start | bytes 21512 | tf_op jit(solution)/shard_map/ppermute | solution.py:13
